TPU v7x, 128 devices: a whole 4x4x4 slice. The times are simulated.
128 devices in a mesh: dp: 4 (over x), seq: 32 (over z, y, core).
Axes of the slice: x: 4, y: 4, z: 4, core: 2. Of those that a mesh axis runs over, the one named last changes fastest.
Arguments:
- inputs: bfloat16 [4, 4096, 960], P('dp', 'seq'), may hold values from -6 to 6
- w_project: bfloat16 [2, 960, 1600], P(None, 'dp', 'seq'), may hold values from -0.1875 to 0.1875
- w_output: bfloat16 [2, 960, 960], P(None, 'dp', 'seq'), may hold values from -1.5 to 1.5
- w_expand: bfloat16 [2, 960, 5120], P(None, 'dp', 'seq'), may hold values from -0.1875 to 0.1875
- w_contract: bfloat16 [2, 2560, 960], P(None, 'dp', 'seq'), may hold values from -0.125 to 0.125
- norm_gains: bfloat16 [3840], P(('dp', 'seq')), may hold values from 0.5 to 1.5
- segments: int32 [4, 4096], P('dp', 'seq'), may hold values from 0 to 20, as said below
- cotangent: bfloat16 [4, 4096, 960], P('dp', 'seq'), may hold values from -6 to 6
Outputs:
- block_output: bfloat16 [4, 4096, 960], P('dp', 'seq')
- input_gradient: float32 [4, 4096, 960], P('dp', 'seq')
- project_gradient: float32 [2, 960, 1600], P(None, 'dp', 'seq')
- output_gradient: float32 [2, 960, 960], P(None, 'dp', 'seq')
- expand_gradient: float32 [2, 960, 5120], P(None, 'dp', 'seq')
- contract_gradient: float32 [2, 2560, 960], P(None, 'dp', 'seq')
- gains_gradient: float32 [3840], P(('dp', 'seq'))
Inputs may be any that keep to these rules, and one draw needn't show every extreme that they name: `segments`: in each sequence the documents are numbered 0, 1, 2, ... in order of position, none empty. In one sequence of each draw, document 0 ends within the first 128 positions, document 1 runs to within the last 128 positions and document 2 fills the rest. In the sequence after it (cyclically) every document has max(200, 2) positions, except the last, which is cut at the sequence's end. In every other sequence the documents have max(200, 2) to 2000 positions each, except the last, which is cut at the sequence's end.
All inputs are finite; a program needn't handle non-finite values.
Results may differ from a plain program's by a relative error of at most 0.03.
Values may be sent and summed in bfloat16 or wider, within the bound.
No kernel may reach another device: no remote copies, remote signals or barrier semaphores. Data moves between devices by JAX's collectives and lax.ppermute only.
A program may use at most 192 MiB of HBM per device.

v0:
```python
import math

import jax
import jax.numpy as jnp
from jax import lax
from jax.sharding import PartitionSpec as P

HEADS = 15
KV_HEADS = 5
HEAD = 64


EPSILON = 1e-05
THETA = 100000.0
MASKED = -1e30


def frequencies(size):
    half = size // 2
    return 1.0 / THETA ** (jnp.arange(half, dtype=jnp.float32) * 2.0 / size)


def rotate(values, cosine, sine):
    half = values.shape[-1] // 2
    first = values[..., :half]
    second = values[..., half:]
    return jnp.concatenate(
        [first * cosine - second * sine, second * cosine + first * sine], axis=-1
    )


def root_norm(stream, gain):
    scale = lax.rsqrt(jnp.mean(stream * stream, axis=-1, keepdims=True) + EPSILON)
    return stream * scale * gain


def gated_unit(gate_up):
    width = gate_up.shape[-1] // 2
    gate = gate_up[..., :width]
    return gate / (1.0 + jnp.exp(-gate)) * gate_up[..., width:]


def plain_dot(left, right):
    return jnp.dot(left, right, preferred_element_type=jnp.float32)


def contract_rows(left, right):
    return lax.dot_general(
        left, right, (((0,), (0,)), ((), ())), preferred_element_type=jnp.float32
    )


def contract_cols(left, right):
    return lax.dot_general(
        left, right, (((1,), (1,)), ((), ())), preferred_element_type=jnp.float32
    )


def fetch_weights(w_project, w_output, w_expand, w_contract, norm_gains, layer):
    project_part, output_part, expand_part, contract_part, gains_part = (
        lax.all_gather(w_project[layer], "seq", axis=1, tiled=True),
        lax.all_gather(w_output[layer], "seq", axis=1, tiled=True),
        lax.all_gather(w_expand[layer], "seq", axis=1, tiled=True),
        lax.all_gather(w_contract[layer], "seq", axis=1, tiled=True),
        lax.all_gather(norm_gains, "seq", axis=0, tiled=True),
    )
    return (
        lax.all_gather(project_part, "dp", axis=0, tiled=True),
        lax.all_gather(output_part, "dp", axis=0, tiled=True),
        lax.all_gather(expand_part, "dp", axis=0, tiled=True),
        lax.all_gather(contract_part, "dp", axis=0, tiled=True),
        lax.all_gather(gains_part, "dp", axis=0, tiled=True),
    )


def fetch_again(w_project, w_output, w_expand, w_contract, norm_gains, layer):
    project_part, output_part, expand_part, contract_part, gains_part = (
        lax.all_gather(w_project[layer], "seq", axis=1, tiled=True),
        lax.all_gather(w_output[layer], "seq", axis=1, tiled=True),
        lax.all_gather(w_expand[layer], "seq", axis=1, tiled=True),
        lax.all_gather(w_contract[layer], "seq", axis=1, tiled=True),
        lax.all_gather(norm_gains, "seq", axis=0, tiled=True),
    )
    return (
        lax.all_gather(project_part, "dp", axis=0, tiled=True),
        lax.all_gather(output_part, "dp", axis=0, tiled=True),
        lax.all_gather(expand_part, "dp", axis=0, tiled=True),
        lax.all_gather(contract_part, "dp", axis=0, tiled=True),
        lax.all_gather(gains_part, "dp", axis=0, tiled=True),
    )


def split_heads(queries, packed, tok_rows):
    group = HEADS // KV_HEADS
    key_width = KV_HEADS * HEAD
    length = packed.shape[0]
    query_groups = (
        queries.reshape(tok_rows, KV_HEADS, group, HEAD)
        .transpose(1, 2, 0, 3)
        .reshape(KV_HEADS, group * tok_rows, HEAD)
    )
    key_groups = packed[:, :key_width].reshape(length, KV_HEADS, HEAD).transpose(1, 0, 2)
    value_groups = packed[:, key_width:].reshape(length, KV_HEADS, HEAD).transpose(1, 0, 2)
    return (query_groups, key_groups, value_groups)


def join_heads(grouped, tok_rows):
    group = HEADS // KV_HEADS
    return (
        grouped.reshape(KV_HEADS, group, tok_rows, HEAD)
        .transpose(2, 0, 1, 3)
        .reshape(tok_rows, HEADS * HEAD)
    )


def attend_forward(queries, packed, mask_rows, tok_rows):
    scale = 1.0 / math.sqrt(HEAD)
    query_groups, key_groups, value_groups = split_heads(queries, packed, tok_rows)

    def one_group(pieces):
        query_group, key_group, value_group = pieces
        scores = jnp.where(mask_rows, contract_cols(query_group, key_group) * scale, MASKED)
        top = jnp.max(scores, axis=1, keepdims=True)
        raised = jnp.exp(scores - top)
        total = jnp.sum(raised, axis=1, keepdims=True)
        chance = (raised / total).astype(jnp.bfloat16)
        return (plain_dot(chance, value_group), top[:, 0] + jnp.log(total[:, 0]))

    mixed, log_total = lax.map(one_group, (query_groups, key_groups, value_groups))
    return (join_heads(mixed, tok_rows), log_total)


def attend_backward(queries, packed, mask_rows, log_total, grad_mixed, tok_rows):
    scale = 1.0 / math.sqrt(HEAD)
    group = HEADS // KV_HEADS
    key_width = KV_HEADS * HEAD
    length = packed.shape[0]
    query_groups, key_groups, value_groups = split_heads(queries, packed, tok_rows)
    grad_groups = (
        grad_mixed.reshape(tok_rows, KV_HEADS, group, HEAD)
        .transpose(1, 2, 0, 3)
        .reshape(KV_HEADS, group * tok_rows, HEAD)
    )

    def one_group(pieces):
        query_group, key_group, value_group, grad_group, total_group = pieces
        scores = jnp.where(mask_rows, contract_cols(query_group, key_group) * scale, MASKED)
        chance = jnp.exp(scores - total_group[:, None])
        grad_chance = contract_cols(grad_group, value_group)
        inner = jnp.sum(chance * grad_chance, axis=1, keepdims=True)
        grad_scores = (chance * (grad_chance - inner)).astype(jnp.bfloat16)
        grad_query = plain_dot(grad_scores, key_group) * scale
        grad_key = contract_rows(grad_scores, query_group) * scale
        grad_value = contract_rows(chance.astype(jnp.bfloat16), grad_group)
        return (grad_query, grad_key, grad_value)

    grad_query, grad_key, grad_value = lax.map(
        one_group, (query_groups, key_groups, value_groups, grad_groups, log_total)
    )
    key_part = grad_key.transpose(1, 0, 2).reshape(length, key_width)
    value_part = grad_value.transpose(1, 0, 2).reshape(length, key_width)
    grad_query = join_heads(grad_query, tok_rows).reshape(tok_rows, HEADS, HEAD)
    return (grad_query, jnp.concatenate([key_part, value_part], axis=1))


def on_device(inputs, w_project, w_output, w_expand, w_contract, norm_gains, segments, cotangent):
    tok_rows = inputs.shape[1]
    width = inputs.shape[2]
    layers = w_project.shape[0]
    key_width = KV_HEADS * HEAD
    group = HEADS // KV_HEADS
    local_segment = segments[0]
    all_segment = lax.all_gather(local_segment, "seq", axis=0, tiled=True)
    length = all_segment.shape[0]
    query_index = lax.axis_index("seq") * tok_rows + jnp.arange(tok_rows, dtype=jnp.int32)
    key_index = jnp.arange(length, dtype=jnp.int32)
    starts = jnp.sum((all_segment[None, :] < local_segment[:, None]).astype(jnp.int32), axis=1)
    position = (query_index - starts).astype(jnp.float32)
    angle = position[:, None] * frequencies(HEAD)[None, :]
    cosine = jnp.cos(angle)[:, None, :]
    sine = jnp.sin(angle)[:, None, :]
    allowed = (local_segment[:, None] == all_segment[None, :]) & (
        query_index[:, None] >= key_index[None, :]
    )
    mask_rows = jnp.tile(allowed, (group, 1))
    stream = inputs[0].astype(jnp.float32)
    records = []
    held = []
    for layer in range(layers):
        fetched = fetch_weights(w_project, w_output, w_expand, w_contract, norm_gains, layer)
        held.append(fetched)
        project, output, expand, contract, gains = fetched
        gain_attend = gains[2 * layer * width : (2 * layer + 1) * width].astype(jnp.float32)
        gain_feed = gains[(2 * layer + 1) * width : (2 * layer + 2) * width].astype(jnp.float32)
        normed = root_norm(stream, gain_attend).astype(jnp.bfloat16)
        projected = plain_dot(normed, project)
        queries = rotate(projected[:, :width].reshape(tok_rows, HEADS, HEAD), cosine, sine).astype(
            jnp.bfloat16
        )
        keys = rotate(
            projected[:, width : width + key_width].reshape(tok_rows, KV_HEADS, HEAD), cosine, sine
        ).astype(jnp.bfloat16)
        values = projected[:, width + key_width :].astype(jnp.bfloat16)
        packed = lax.all_gather(
            jnp.concatenate([keys.reshape(tok_rows, key_width), values], axis=1),
            "seq",
            axis=0,
            tiled=True,
        )
        mixed, log_total = attend_forward(queries, packed, mask_rows, tok_rows)
        mixed = mixed.astype(jnp.bfloat16)
        middle = stream + plain_dot(mixed, output)
        normed_feed = root_norm(middle, gain_feed).astype(jnp.bfloat16)
        gate_up = plain_dot(normed_feed, expand)
        hidden = gated_unit(gate_up).astype(jnp.bfloat16)
        records.append(
            (
                stream,
                normed,
                queries,
                packed,
                log_total,
                mixed,
                middle,
                normed_feed,
                gate_up,
                hidden,
            )
        )
        stream = middle + plain_dot(hidden, contract)
    block_output = stream.astype(jnp.bfloat16)[None]
    grad_stream = cotangent[0].astype(jnp.float32)
    project_list = [None] * layers
    output_list = [None] * layers
    expand_list = [None] * layers
    contract_list = [None] * layers
    gains_total = jnp.zeros((norm_gains.shape[0],), jnp.float32)
    for layer in reversed(range(layers)):
        project, output, expand, contract, gains = fetch_again(
            w_project, w_output, w_expand, w_contract, norm_gains, layer
        )
        (
            stream_in,
            normed,
            queries,
            packed,
            log_total,
            mixed,
            middle,
            normed_feed,
            gate_up,
            hidden,
        ) = records[layer]
        gain_attend = gains[2 * layer * width : (2 * layer + 1) * width].astype(jnp.float32)
        gain_feed = gains[(2 * layer + 1) * width : (2 * layer + 2) * width].astype(jnp.float32)
        grad_low = grad_stream.astype(jnp.bfloat16)
        grad_contract = contract_rows(hidden, grad_low)
        grad_hidden = contract_cols(grad_low, contract)
        grad_gate_up = jax.vjp(gated_unit, gate_up)[1](grad_hidden)[0].astype(jnp.bfloat16)
        grad_expand = contract_rows(normed_feed, grad_gate_up)
        grad_feed = contract_cols(grad_gate_up, expand)
        grad_middle_part, grad_gain_feed = jax.vjp(root_norm, middle, gain_feed)[1](grad_feed)
        grad_middle = grad_stream + grad_middle_part
        grad_middle_low = grad_middle.astype(jnp.bfloat16)
        grad_output = contract_rows(mixed, grad_middle_low)
        grad_mixed = contract_cols(grad_middle_low, output).astype(jnp.bfloat16)
        grad_query, grad_packed = attend_backward(
            queries, packed, mask_rows, log_total, grad_mixed, tok_rows
        )
        grad_local = lax.psum_scatter(
            grad_packed.astype(jnp.bfloat16), "seq", scatter_dimension=0, tiled=True
        ).astype(jnp.float32)
        grad_query = rotate(grad_query, cosine, -sine)
        grad_key = rotate(
            grad_local[:, :key_width].reshape(tok_rows, KV_HEADS, HEAD), cosine, -sine
        )
        grad_projected = jnp.concatenate(
            [
                grad_query.reshape(tok_rows, width),
                grad_key.reshape(tok_rows, key_width),
                grad_local[:, key_width:],
            ],
            axis=1,
        ).astype(jnp.bfloat16)
        grad_project = contract_rows(normed, grad_projected)
        grad_normed = contract_cols(grad_projected, project)
        grad_input_part, grad_gain_attend = jax.vjp(root_norm, stream_in, gain_attend)[1](
            grad_normed
        )
        grad_stream = grad_middle + grad_input_part
        gains_full = (
            jnp.zeros((gains.shape[0],), jnp.float32)
            .at[2 * layer * width : (2 * layer + 2) * width]
            .set(jnp.concatenate([grad_gain_attend, grad_gain_feed]))
        )
        part_project, part_output, part_expand, part_contract, part_gains = (
            lax.psum_scatter(
                grad_project.astype(jnp.bfloat16), "dp", scatter_dimension=0, tiled=True
            ).astype(jnp.float32),
            lax.psum_scatter(
                grad_output.astype(jnp.bfloat16), "dp", scatter_dimension=0, tiled=True
            ).astype(jnp.float32),
            lax.psum_scatter(
                grad_expand.astype(jnp.bfloat16), "dp", scatter_dimension=0, tiled=True
            ).astype(jnp.float32),
            lax.psum_scatter(
                grad_contract.astype(jnp.bfloat16), "dp", scatter_dimension=0, tiled=True
            ).astype(jnp.float32),
            lax.psum_scatter(
                gains_full.astype(jnp.bfloat16), "dp", scatter_dimension=0, tiled=True
            ).astype(jnp.float32),
        )
        part_project, part_output, part_expand, part_contract, part_gains = (
            lax.psum_scatter(
                part_project.astype(jnp.bfloat16), "seq", scatter_dimension=1, tiled=True
            ).astype(jnp.float32),
            lax.psum_scatter(
                part_output.astype(jnp.bfloat16), "seq", scatter_dimension=1, tiled=True
            ).astype(jnp.float32),
            lax.psum_scatter(
                part_expand.astype(jnp.bfloat16), "seq", scatter_dimension=1, tiled=True
            ).astype(jnp.float32),
            lax.psum_scatter(
                part_contract.astype(jnp.bfloat16), "seq", scatter_dimension=1, tiled=True
            ).astype(jnp.float32),
            lax.psum_scatter(
                part_gains.astype(jnp.bfloat16), "seq", scatter_dimension=0, tiled=True
            ).astype(jnp.float32),
        )
        project_list[layer] = part_project
        output_list[layer] = part_output
        expand_list[layer] = part_expand
        contract_list[layer] = part_contract
        gains_total = gains_total + part_gains
    return (
        block_output,
        grad_stream[None],
        jnp.stack(project_list),
        jnp.stack(output_list),
        jnp.stack(expand_list),
        jnp.stack(contract_list),
        gains_total,
    )


def solution(mesh):
    in_specs = (
        P("dp", "seq", None),
        P(None, "dp", "seq"),
        P(None, "dp", "seq"),
        P(None, "dp", "seq"),
        P(None, "dp", "seq"),
        P(("dp", "seq")),
        P("dp", "seq"),
        P("dp", "seq", None),
    )
    out_specs = (
        P("dp", "seq", None),
        P("dp", "seq", None),
        P(None, "dp", "seq"),
        P(None, "dp", "seq"),
        P(None, "dp", "seq"),
        P(None, "dp", "seq"),
        P(("dp", "seq")),
    )
    return jax.shard_map(
        on_device, mesh=mesh, in_specs=in_specs, out_specs=out_specs, check_vma=False
    )
```

profile of v0, /device:TPU:1, one launch (start us, length us, event | category | flops | bytes accessed | tf_op | source)
XLA Modules:
  0.0 1885.3 jit_solution(1654894846319965861)
XLA Ops:
  8.3 28.6 %all-gather = bf16[1,240,1600]{1,0,2:T(2,128)(2,1)S(1)} all-gather(bf16[1,240,50]{1,0,2:T(2,128)(2,1)S(1)} %get-tuple-element.472), channel_id=2, replica_groups=mesh['dp'=4,'seq'=32] {'seq'}, dimensions={2}, use_global_device_ids=true | all-gather | bytes 792000 | tf_op jit(solution)/shard_map/all_gather | solution.py:61
  44.7 62.2 %all-reduce.6 = bf16[960]{0:T(1024)(128)(2,1)S(1)} all-reduce(bf16[960]{0:T(1024)(128)(2,1)S(1)} %dynamic-update-slice.4), channel_id=1, replica_groups=mesh['dp'=4,'seq'=32] {'seq'}, use_global_device_ids=true, to_apply=%add.6 | all-reduce | flops 960 | bytes 3840
  107.1 20.4 %all-gather.2 = s32[1,4096]{1,0:T(1,128)S(1)} all-gather(s32[1,128]{1,0:T(1,128)S(1)} %copy-done.68), channel_id=4, replica_groups=mesh['dp'=4,'seq'=32] {'seq'}, dimensions={1}, use_global_device_ids=true | all-gather | bytes 16896 | tf_op jit(solution)/shard_map/all_gather | solution.py:173
  142.6 28.0 %all-gather.3 = bf16[1,240,960]{1,0,2:T(2,128)(2,1)S(1)} all-gather(bf16[1,240,30]{1,0,2:T(2,128)(2,1)S(1)} %get-tuple-element.474), channel_id=5, replica_groups=mesh['dp'=4,'seq'=32] {'seq'}, dimensions={2}, use_global_device_ids=true | all-gather | bytes 475200 | tf_op jit(solution)/shard_map/all_gather | solution.py:62
  180.3 23.8 %all-gather.9 = bf16[1,240,1600]{1,0,2:T(2,128)(2,1)S(1)} all-gather(bf16[1,240,50]{1,0,2:T(2,128)(2,1)S(1)} %get-tuple-element.471), channel_id=11, replica_groups=mesh['dp'=4,'seq'=32] {'seq'}, dimensions={2}, use_global_device_ids=true | all-gather | bytes 792000 | tf_op jit(solution)/shard_map/all_gather | solution.py:61
  209.4 10.6 all-gather.34.cloned.1.call-start
  242.8 35.3 %while.58 = (s32[]{:T(128)}, bf16[5,384,64]{1,2,0:T(8,128)(2,1)}, f32[5,384]{1,0:T(8,128)S(1)}, bf16[5,384,64]{2,1,0:T(8,128)(2,1)}, bf16[5,4096,64]{2,1,0:T(8,1...) while((s32[]{:T(128)}, bf16[5,384,64]{1,2,0:T(8,128)(2,1)}, ...), condition=%wide.region_5.6_spmd.clone, body=%wide.region_2.5_spmd.clone.sunk | while | flops 415235712 | bytes 21713000 | solution.py:129
  281.9 73.5 %all-gather.42.cloned.1.call-done = bf16[1,960,5120]{2,1,0:T(8,128)(2,1)} async-done(((bf16[1,240,5120]{2,1,0:T(8,128)(2,1)}), bf16[1,960,5120]{2,1,0:T(8,128)(2,1)}) %all-gather.42.cloned.1.call-update) | async-done | bytes 9830416 | tf_op jit(solution)/shard_map/all_gather | solution.py:70
  362.8 49.5 %all-gather.46.cloned.1.call-done = bf16[1,2560,960]{1,2,0:T(8,128)(2,1)} async-done(((bf16[1,640,960]{1,2,0:T(8,128)(2,1)}), bf16[1,2560,960]{1,2,0:T(8,128)(2,1)}) %all-gather.46.cloned.1.call-update) | async-done | bytes 4915216 | tf_op jit(solution)/shard_map/all_gather | solution.py:71
  416.2 38.2 %all-gather.48.cloned.1.call-done = bf16[1,960,1600]{2,1,0:T(8,128)(2,1)} async-done(((bf16[1,240,1600]{2,1,0:T(8,128)(2,1)}), bf16[1,960,1600]{2,1,0:T(8,128)(2,1)}) %all-gather.48.cloned.1.call-update) | async-done | bytes 3072016 | tf_op jit(solution)/shard_map/all_gather | solution.py:68
  458.7 25.7 %all-gather.11 = bf16[1,240,960]{1,0,2:T(2,128)(2,1)S(1)} all-gather(bf16[1,240,30]{1,0,2:T(2,128)(2,1)S(1)} %get-tuple-element.473), channel_id=13, replica_groups=mesh['dp'=4,'seq'=32] {'seq'}, dimensions={2}, use_global_device_ids=true | all-gather | bytes 475200 | tf_op jit(solution)/shard_map/all_gather | solution.py:62
  486.6 15.9 all-gather.52.cloned.1.call-done
  507.0 41.5 %all-gather.56.cloned.1.call-done = bf16[1,640,960]{1,0,2:T(2,128)(2,1)} async-done(((bf16[1,640,30]{1,0,2:T(2,128)(2,1)}), bf16[1,640,960]{1,0,2:T(2,128)(2,1)}) %all-gather.56.cloned.1.call-update) | async-done | bytes 1228816 | tf_op jit(solution)/shard_map/all_gather | solution.py:64
  551.9 50.5 %all-gather.34.cloned.1.call-done = bf16[4096,640]{0,1:T(8,128)(2,1)} async-done(((bf16[128,640]{0,1:T(8,128)(2,1)}), bf16[4096,640]{0,1:T(8,128)(2,1)}) %all-gather.34.cloned.1.call-update) | async-done | bytes 5242896 | tf_op jit(solution)/shard_map/all_gather | solution.py:204
  620.3 32.3 %while.59 = (s32[]{:T(128)}, bf16[5,384,64]{1,2,0:T(8,128)(2,1)S(1)}, f32[5,384]{1,0:T(8,128)S(1)}, bf16[5,384,64]{2,1,0:T(8,128)(2,1)S(1)}, bf16[5,4096,64]{2,1...) while((s32[]{:T(128)}, ...), condition=%wide.region_11.12_spmd.clone, body=%wide.region_8.11_spmd.clone.sunk | while | flops 415235712 | bytes 21714024 | solution.py:129
  655.3 74.4 %all-gather.54.cloned.1.call-done = bf16[1,960,5120]{2,1,0:T(8,128)(2,1)} async-done(((bf16[1,240,5120]{2,1,0:T(8,128)(2,1)}), bf16[1,960,5120]{2,1,0:T(8,128)(2,1)}) %all-gather.54.cloned.1.call-update) | async-done | bytes 9830416 | tf_op jit(solution)/shard_map/all_gather | solution.py:70
  736.8 49.7 %all-gather.58.cloned.1.call-done = bf16[1,2560,960]{1,2,0:T(8,128)(2,1)} async-done(((bf16[1,640,960]{1,2,0:T(8,128)(2,1)}), bf16[1,2560,960]{1,2,0:T(8,128)(2,1)}) %all-gather.58.cloned.1.call-update) | async-done | bytes 4915216 | tf_op jit(solution)/shard_map/all_gather | solution.py:71
  801.0 61.5 %while.60 = (s32[]{:T(128)}, f32[5,384,64]{1,2,0:T(8,128)S(1)}, bf16[5,4096,64]{1,2,0:T(8,128)(2,1)}, bf16[5,4096,64]{1,2,0:T(8,128)(2,1)}, bf16[5,384,64]{2,1,0...) while((s32[]{:T(128)}, f32[5,384,64]{1,2,0:T(8,128)S(1)}, ...), condition=%wide.region_16.17_spmd.clone, body=%wide.region_14.16_spmd.clone.sunk | while | flops 1021075072 | bytes 74429616 | solution.py:157
  876.7 83.0 %reduce-scatter.45.cloned.1.call-done = bf16[128,640]{1,0:T(8,128)(2,1)} async-done(((bf16[4096,640]{1,0:T(8,128)(2,1)}), bf16[128,640]{1,0:T(8,128)(2,1)}) %reduce-scatter.45.cloned.1.call-update) | async-done | bytes 163856
  980.0 73.3 %while.61 = (s32[]{:T(128)}, f32[5,384,64]{1,2,0:T(8,128)}, bf16[5,4096,64]{1,2,0:T(8,128)(2,1)}, bf16[5,4096,64]{1,2,0:T(8,128)(2,1)}, bf16[5,384,64]{2,1,0:T(8...) while((s32[]{:T(128)}, f32[5,384,64]{1,2,0:T(8,128)}, ...), condition=%wide.region_22.23_spmd.clone, body=%wide.region_20.22_spmd.clone.sunk | while | flops 1021075072 | bytes 74429104 | solution.py:157
  1077.7 73.0 %reduce-scatter.47.cloned.1.call-done = bf16[128,640]{1,0:T(8,128)(2,1)} async-done(((bf16[4096,640]{1,0:T(8,128)(2,1)}), bf16[128,640]{1,0:T(8,128)(2,1)}) %reduce-scatter.47.cloned.1.call-update) | async-done | bytes 163856
  1195.8 17.3 reduce-scatter.37.cloned.1.call-done
  1213.1 40.9 %reduce-scatter.35.cloned.1.call-done = bf16[240,1600]{1,0:T(8,128)(2,1)} async-done(((bf16[960,1600]{1,0:T(8,128)(2,1)}), bf16[240,1600]{1,0:T(8,128)(2,1)}) %reduce-scatter.35.cloned.1.call-update) | async-done | bytes 768016 | tf_op jit(solution)/shard_map/reduce_scatter | solution.py:297
  1254.0 40.9 %reduce-scatter.33.cloned.1.call-done = bf16[240,1600]{1,0:T(8,128)(2,1)} async-done(((bf16[960,1600]{1,0:T(8,128)(2,1)}), bf16[240,1600]{1,0:T(8,128)(2,1)}) %reduce-scatter.33.cloned.1.call-update) | async-done | bytes 768016 | tf_op jit(solution)/shard_map/reduce_scatter | solution.py:297
  1295.0 94.3 %reduce-scatter.43.cloned.1.call-done = bf16[240,5120]{1,0:T(8,128)(2,1)} async-done(((bf16[960,5120]{1,0:T(8,128)(2,1)}), bf16[240,5120]{1,0:T(8,128)(2,1)}) %reduce-scatter.43.cloned.1.call-update) | async-done | bytes 2457616 | tf_op jit(solution)/shard_map/reduce_scatter | solution.py:303
  1393.7 90.1 %reduce-scatter.41.cloned.1.call-done = bf16[240,5120]{1,0:T(8,128)(2,1)} async-done(((bf16[960,5120]{1,0:T(8,128)(2,1)}), bf16[240,5120]{1,0:T(8,128)(2,1)}) %reduce-scatter.41.cloned.1.call-update) | async-done | bytes 2457616 | tf_op jit(solution)/shard_map/reduce_scatter | solution.py:303
  1495.5 45.9 %reduce-scatter.55.cloned.1.call-done = bf16[640,960]{1,0:T(8,128)(2,1)} async-done(((bf16[2560,960]{1,0:T(8,128)(2,1)}), bf16[640,960]{1,0:T(8,128)(2,1)}) %reduce-scatter.55.cloned.1.call-update) | async-done | bytes 1228816
  1546.7 12.1 all-reduce.22
  1558.9 66.0 %all-reduce.20 = (bf16[960]{0:T(1024)(128)(2,1)S(1)}, bf16[960]{0:T(1024)(128)(2,1)S(1)}) all-reduce(bf16[960]{0:T(1024)(128)(2,1)S(1)} %dynamic-slice.33, bf16[960]{0:T(1024)(128)(2,1)S(1)} %dynamic-slice.29), channel_id=40, replica_groups=mesh['dp'=4,'seq'=32] {'seq'}, use_global_device_ids=true, to_apply=%region_48.49.clone | all-reduce | flops 1920 | bytes 7680
  1628.0 77.0 %fusion.188 = (bf16[640,32]{0,1:T(8,128)(2,1)S(1)}, bf16[640,32]{0,1:T(8,128)(2,1)S(1)}) fusion(bf16[640,960]{0,1:T(8,128)(2,1)S(1)} %copy.146, bf16[640,960]{0,1:T(8,128)(2,1)S(1)} %copy.144), kind=kCustom, calls=%all-reduce-scatter.2 | all-reduce-scatter fusion | flops 1310721 | bytes 2540032
  1719.9 73.7 %reduce-scatter.51.cloned.1.call-done = bf16[160,240]{1,0:T(8,128)(2,1)} async-done(((bf16[5120,240]{1,0:T(8,128)(2,1)}), bf16[160,240]{1,0:T(8,128)(2,1)}) %reduce-scatter.51.cloned.1.call-update) | async-done | bytes 76816
  1794.7 81.6 %reduce-scatter.49.cloned.1.call-done = bf16[160,240]{1,0:T(8,128)(2,1)} async-done(((bf16[5120,240]{1,0:T(8,128)(2,1)}), bf16[160,240]{1,0:T(8,128)(2,1)}) %reduce-scatter.49.cloned.1.call-update) | async-done | bytes 76816
  (559 shorter events, 475.6 us)
Async XLA Ops:
  7.2 130.8 %all-gather.36.cloned.1.call-start = ((), (), s32[]{:S(2)}) async-start(), calls=%async_computation.20 | async-start | bytes 3993600 | tf_op jit(solution)/shard_map/all_gather | solution.py:68
  40.7 132.0 %all-gather.40.cloned.1.call-start = ((), (), s32[]{:S(2)}) async-start(), calls=%async_computation.22 | async-start | bytes 2703360 | tf_op jit(solution)/shard_map/all_gather | solution.py:63
  41.5 135.8 %all-gather.44.cloned.1.call-start = ((), (), s32[]{:S(2)}) async-start(), calls=%async_computation.24 | async-start | bytes 2534400 | tf_op jit(solution)/shard_map/all_gather | solution.py:64
  42.4 185.9 %all-gather.32.cloned.1.call-start = ((), (), s32[]{:S(2)}) async-start(), calls=%async_computation.12 | async-start | bytes 5406720 | tf_op jit(solution)/shard_map/all_gather | solution.py:204
  138.1 413.4 %copy-start.28 = (f32[128,32]{0,1:T(8,128)}, f32[128,32]{0,1:T(8,128)S(1)}, u32[]{:S(2)}) copy-start(f32[128,32]{0,1:T(8,128)S(1)} %get-tuple-element.481) | copy-start | bytes 49156
  142.4 136.9 %all-gather.38.cloned.1.call-start = ((), (), s32[]{:S(2)}) async-start(), calls=%async_computation.21 | async-start | bytes 2457600 | tf_op jit(solution)/shard_map/all_gather | solution.py:69
  172.7 182.7 %all-gather.42.cloned.1.call-start = ((), (), s32[]{:S(2)}) async-start(), calls=%async_computation.23 | async-start | bytes 12288000 | tf_op jit(solution)/shard_map/all_gather | solution.py:70
  177.3 235.0 %all-gather.46.cloned.1.call-start = ((), (), s32[]{:S(2)}) async-start(), calls=%async_computation.25 | async-start | bytes 6144000 | tf_op jit(solution)/shard_map/all_gather | solution.py:71
  180.3 274.1 %all-gather.48.cloned.1.call-start = ((), (), s32[]{:S(2)}) async-start(), calls=%async_computation.26 | async-start | bytes 3993600 | tf_op jit(solution)/shard_map/all_gather | solution.py:68
  208.0 294.5 %all-gather.52.cloned.1.call-start = ((), (), s32[]{:S(2)}) async-start(), calls=%async_computation.28 | async-start | bytes 2703360 | tf_op jit(solution)/shard_map/all_gather | solution.py:63
  208.8 339.7 %all-gather.56.cloned.1.call-start = ((), (), s32[]{:S(2)}) async-start(), calls=%async_computation.30 | async-start | bytes 2534400 | tf_op jit(solution)/shard_map/all_gather | solution.py:64
  209.4 393.1 %all-gather.34.cloned.1.call-start = ((), (), s32[]{:S(2)}) async-start(), calls=%async_computation.13 | async-start | bytes 5406720 | tf_op jit(solution)/shard_map/all_gather | solution.py:204
  458.7 194.1 %all-gather.50.cloned.1.call-start = ((), (), s32[]{:S(2)}) async-start(), calls=%async_computation.27 | async-start | bytes 2457600 | tf_op jit(solution)/shard_map/all_gather | solution.py:69
  486.6 243.2 %all-gather.54.cloned.1.call-start = ((), (), s32[]{:S(2)}) async-start(), calls=%async_computation.29 | async-start | bytes 12288000 | tf_op jit(solution)/shard_map/all_gather | solution.py:70
  507.0 279.5 %all-gather.58.cloned.1.call-start = ((), (), s32[]{:S(2)}) async-start(), calls=%async_computation.31 | async-start | bytes 6144000 | tf_op jit(solution)/shard_map/all_gather | solution.py:71
  551.4 408.2 %reduce-scatter.45.cloned.1.call-start = ((), (), s32[]{:S(2)}) async-start(), calls=%async_computation.32 | async-start | bytes 5406720
  875.9 274.8 %reduce-scatter.47.cloned.1.call-start = ((), (), s32[]{:S(2)}) async-start(), calls=%async_computation.33 | async-start | bytes 5406720
  1066.6 129.1 %reduce-scatter.39.cloned.1.call-start = ((), (), s32[]{:S(2)}) async-start(), calls=%async_computation.17 | async-start | bytes 2457600 | tf_op jit(solution)/shard_map/reduce_scatter | solution.py:300
  1069.5 143.5 %reduce-scatter.37.cloned.1.call-start = ((), (), s32[]{:S(2)}) async-start(), calls=%async_computation.16 | async-start | bytes 2457600 | tf_op jit(solution)/shard_map/reduce_scatter | solution.py:300
  1071.6 182.4 %reduce-scatter.35.cloned.1.call-start = ((), (), s32[]{:S(2)}) async-start(), calls=%async_computation.15 | async-start | bytes 3993600 | tf_op jit(solution)/shard_map/reduce_scatter | solution.py:297
  1074.4 220.5 %reduce-scatter.33.cloned.1.call-start = ((), (), s32[]{:S(2)}) async-start(), calls=%async_computation.14 | async-start | bytes 3993600 | tf_op jit(solution)/shard_map/reduce_scatter | solution.py:297
  1154.9 234.4 %reduce-scatter.43.cloned.1.call-start = ((), (), s32[]{:S(2)}) async-start(), calls=%async_computation.19 | async-start | bytes 12288000 | tf_op jit(solution)/shard_map/reduce_scatter | solution.py:303
  1163.2 320.7 %reduce-scatter.41.cloned.1.call-start = ((), (), s32[]{:S(2)}) async-start(), calls=%async_computation.18 | async-start | bytes 12288000 | tf_op jit(solution)/shard_map/reduce_scatter | solution.py:303
  1170.4 371.0 %reduce-scatter.55.cloned.1.call-start = ((), (), s32[]{:S(2)}) async-start(), calls=%async_computation.37 | async-start | bytes 6553600
  1183.1 442.8 %reduce-scatter.53.cloned.1.call-start = ((), (), s32[]{:S(2)}) async-start(), calls=%async_computation.36 | async-start | bytes 6553600
  1195.7 518.3 %all-reduce.26.cloned.1.call-start = ((), (), s32[]{:S(2)}) async-start(), calls=%async_computation.38 | async-start | bytes 5160960
  1294.9 498.8 %reduce-scatter.51.cloned.1.call-start = ((), (), s32[]{:S(2)}) async-start(), calls=%async_computation.35 | async-start | bytes 2703360
  1393.7 482.6 %reduce-scatter.49.cloned.1.call-start = ((), (), s32[]{:S(2)}) async-start(), calls=%async_computation.34 | async-start | bytes 2703360
  1705.0 7.1 collective-permute-start.2
  1707.0 5.6 collective-permute-start
  1708.9 3.2 collective-permute-start.3
  1710.2 2.4 collective-permute-start.1
  (98 other events, 3134.0 us)
Sparse Core Ops, SparseCore 0:
  40.9 38.6 all-gather.35
  82.4 45.2 all-gather.39
  130.6 44.2 all-gather.43
  177.0 51.2 all-gather.31
  229.8 28.7 all-gather.37
  260.1 95.2 all-gather.41
  357.1 55.1 all-gather.45
  413.9 40.4 all-gather.47
  457.2 45.2 all-gather.51
  504.7 43.7 all-gather.55
  551.3 51.1 all-gather.33
  604.0 28.7 all-gather.49
  634.4 95.2 all-gather.53
  731.3 55.1 all-gather.57
  876.0 83.6 reduce-scatter.44
  1066.7 83.9 reduce-scatter.46
  1153.0 29.4 reduce-scatter.38
  1184.8 28.2 reduce-scatter.36
  1215.5 38.4 reduce-scatter.34
  1256.4 38.4 reduce-scatter.32
  1297.4 91.8 reduce-scatter.42
  1391.9 91.8 reduce-scatter.40
  1486.3 55.1 reduce-scatter.54
  1543.7 55.3 reduce-scatter.52
  1602.9 109.4 all-reduce.25
  1715.8 77.8 reduce-scatter.50
  1797.5 78.7 reduce-scatter.48
where the time goes:
time: 1900 us; the launch traced here: 1890 us
  waiting for transfers between devices  1040 us (55%)
  blocking collectives  352 us (19%)
  matrix products  259 us (14%)
  local copies, waits for them, and re-layouts  146 us (8%)
  other arithmetic  46.1 us (2%)
  between operations  20 us (1%)
    unnamed x38, waiting for transfers between devices  359 us
    unnamed x5, blocking collectives  226 us
    reduce_scatter x2, waiting for transfers between devices, on_device(): lax.psum_scatter(grad_expand.astype(jnp.bfloat16), 'dp', scatter_dimensio...  184 us
    all_gather x2, waiting for transfers between devices, fetch_weights(): lax.all_gather(expand_part, 'dp', axis=0, tiled=True)  148 us
    dot_general x38, matrix products, contract_cols(): lax.dot_general(left, right, (((1,), (1,)), ((), ())), preferred_element_...  109 us
    all_gather x2, waiting for transfers between devices, fetch_weights(): lax.all_gather(contract_part, 'dp', axis=0, tiled=True)  99.2 us
    dot_general x28, matrix products, plain_dot(): return jnp.dot(left, right, preferred_element_type=jnp.float32)  91.2 us
    reduce_scatter x2, waiting for transfers between devices, on_device(): lax.psum_scatter(grad_project.astype(jnp.bfloat16), 'dp', scatter_dimensi...  81.8 us
  transfers between devices with their start and end apart: 31, of which 19 were waited for; matrix products, arithmetic and copies ran while one was open for 17% of the time, Pallas kernels for 0%

commit v1 on v0

v1 whole, which is shorter than its diff:
```python
import math

import jax
import jax.numpy as jnp
from jax import lax
from jax.experimental import pallas as pl
from jax.experimental.pallas import tpu as pltpu
from jax.sharding import PartitionSpec as P

HEADS = 15
KV_HEADS = 5
HEAD = 64
GROUP = HEADS // KV_HEADS
KVD = KV_HEADS * HEAD

EPSILON = 1e-05
THETA = 100000.0
MASKED = -1e30

RING_Y = [[z * 8 + y * 2 + c for y in range(4)] for z in range(4) for c in range(2)]
RING_Z = [[z * 8 + y * 2 + c for z in range(4)] for y in range(4) for c in range(2)]
PLANE = [[i * 2 + c for i in range(16)] for c in range(2)]
SWAP = [(i, i ^ 1) for i in range(32)]

R_EXPAND = 160
R_PROJECT = 64
R_OUTPUT = 32
R_CONTRACT = 96


def frequencies(size):
    half = size // 2
    return 1.0 / THETA ** (jnp.arange(half, dtype=jnp.float32) * 2.0 / size)


def rotate(values, cosine, sine):
    half = values.shape[-1] // 2
    first = values[..., :half]
    second = values[..., half:]
    return jnp.concatenate(
        [first * cosine - second * sine, second * cosine + first * sine], axis=-1
    )


def root_norm(stream, gain):
    scale = lax.rsqrt(jnp.mean(stream * stream, axis=-1, keepdims=True) + EPSILON)
    return stream * scale * gain


def gated_unit(gate_up):
    width = gate_up.shape[-1] // 2
    gate = gate_up[..., :width]
    return gate / (1.0 + jnp.exp(-gate)) * gate_up[..., width:]


def plain_dot(left, right):
    return jnp.dot(left, right, preferred_element_type=jnp.float32)


def contract_rows(left, right):
    return lax.dot_general(
        left, right, (((0,), (0,)), ((), ())), preferred_element_type=jnp.float32
    )


def contract_cols(left, right):
    return lax.dot_general(
        left, right, (((1,), (1,)), ((), ())), preferred_element_type=jnp.float32
    )


def pad_rows(array, rows, axis):
    widths = [(0, 0)] * array.ndim
    widths[axis] = (0, rows - array.shape[axis])
    return jnp.pad(array, widths)


def swap_cores(array):
    return lax.ppermute(array, "seq", SWAP)


def gather_seq(array):
    along_y = lax.all_gather(array, "seq", axis_index_groups=RING_Y)
    plane = lax.all_gather(along_y, "seq", axis_index_groups=RING_Z)
    other = swap_cores(plane)
    core = lax.axis_index("seq") % 2
    first = jnp.where(core == 0, plane, other)
    second = jnp.where(core == 0, other, plane)
    return jnp.stack([first, second], axis=2).reshape((32,) + array.shape)


def reduce_seq(array):
    pairs = array.reshape((16, 2) + array.shape[1:])
    core = lax.axis_index("seq") % 2
    mine = jnp.where(core == 0, pairs[:, 0], pairs[:, 1])
    theirs = jnp.where(core == 0, pairs[:, 1], pairs[:, 0])
    arrived = swap_cores(theirs)
    both = (mine.astype(jnp.float32) + arrived.astype(jnp.float32)).astype(jnp.bfloat16)
    spread = lax.all_to_all(both, "seq", 0, 0, axis_index_groups=PLANE, tiled=True)
    return jnp.sum(spread.astype(jnp.float32), axis=0)


def reduce_dp(array):
    rows = array.shape[0]
    parts = array.reshape(rows, 4, 240).transpose(1, 0, 2).astype(jnp.bfloat16)
    spread = lax.all_to_all(parts, "dp", 0, 0, tiled=True)
    return jnp.sum(spread.astype(jnp.float32), axis=0)


def reduce_bulk(array):
    narrow = R_EXPAND + R_OUTPUT
    first = array[:narrow].reshape(narrow, 4, 240).transpose(1, 0, 2)
    last = array[narrow:].reshape(3, 32, 960).transpose(1, 0, 2).reshape(32, 2880)[:, :2560]
    last = last.reshape(32, 4, 640).transpose(1, 0, 2)
    last = jnp.pad(last, ((0, 0), (0, 0), (0, 80))).reshape(4, R_CONTRACT, 240)
    parts = jnp.concatenate([first, last], axis=1).astype(jnp.bfloat16)
    spread = lax.all_to_all(parts, "dp", 0, 0, tiled=True)
    return jnp.sum(spread.astype(jnp.float32), axis=0)


def gather_dp(array):
    parts = lax.all_gather(array, "dp")
    return parts.transpose(1, 0, 2).reshape(array.shape[0], 4 * array.shape[1])


def pack_contract(rows):
    wide = jnp.pad(rows, ((0, 0), (0, 320)))
    return wide.reshape(32, 3, 960).transpose(1, 0, 2).reshape(R_CONTRACT, 960)


def unpack_contract(block):
    wide = block.reshape(32, 3, 32, 960).transpose(0, 2, 1, 3).reshape(32, 32, 2880)
    return wide[:, :30, :2560].reshape(960, 2560)


def spread_contract(grad):
    wide = jnp.pad(grad.reshape(32, 30, 2560), ((0, 0), (0, 2), (0, 320)))
    return wide.reshape(32, 32, 3, 960).transpose(0, 2, 1, 3).reshape(32, R_CONTRACT, 960)


CHUNK = 512


def nt_dot(left, right):
    return lax.dot_general(
        left, right, (((1,), (1,)), ((), ())), preferred_element_type=jnp.float32
    )


def tn_dot(left, right):
    return lax.dot_general(
        left, right, (((0,), (0,)), ((), ())), preferred_element_type=jnp.float32
    )


def take_heads(ref, head):
    return jnp.concatenate(
        [ref[:, (GROUP * head + g) * HEAD : (GROUP * head + g + 1) * HEAD] for g in range(GROUP)],
        axis=0,
    )


def take_row(ref, head):
    return jnp.concatenate(
        [ref[GROUP * head + g : GROUP * head + g + 1, :] for g in range(GROUP)], axis=1
    )


def forward_kernel(range_ref, query_ref, packed_ref, bias_ref, mixed_ref, total_ref):
    tok_rows = query_ref.shape[0]
    lanes = GROUP * tok_rows
    low, high = range_ref[0], range_ref[1]
    for head in range(KV_HEADS):
        query = take_heads(query_ref, head)

        def step(index, carry, head=head, query=query):
            top, total, mixed = carry
            rows = pl.ds(pl.multiple_of(index * CHUNK, CHUNK), CHUNK)
            key = packed_ref[rows, head * HEAD : (head + 1) * HEAD]
            value = packed_ref[rows, KVD + head * HEAD : KVD + (head + 1) * HEAD]
            bias = bias_ref[rows, :]
            scores = nt_dot(key, query) + jnp.concatenate([bias] * GROUP, axis=1)
            new_top = jnp.maximum(top, jnp.max(scores, axis=0, keepdims=True))
            raised = jnp.exp(scores - new_top)
            shrink = jnp.exp(top - new_top)
            total = total * shrink + jnp.sum(raised, axis=0, keepdims=True)
            mixed = mixed * shrink + tn_dot(value, raised.astype(jnp.bfloat16))
            return new_top, total, mixed

        start = (
            jnp.full((1, lanes), MASKED, jnp.float32),
            jnp.zeros((1, lanes), jnp.float32),
            jnp.zeros((HEAD, lanes), jnp.float32),
        )
        top, total, mixed = lax.fori_loop(low, high, step, start)
        mixed = mixed / total
        log_total = top + jnp.log(total)
        for g in range(GROUP):
            at = GROUP * head + g
            columns = slice(g * tok_rows, (g + 1) * tok_rows)
            mixed_ref[at * HEAD : (at + 1) * HEAD, :] = mixed[:, columns]
            total_ref[at : at + 1, :] = log_total[:, columns]


def backward_kernel(
    range_ref, query_ref, packed_ref, bias_ref, total_ref, inner_ref, grad_ref, query_out, packed_out
):
    tok_rows = query_ref.shape[0]
    low, high = range_ref[0], range_ref[1]
    packed_out[...] = jnp.zeros(packed_out.shape, packed_out.dtype)
    for head in range(KV_HEADS):
        query = take_heads(query_ref, head)
        grad = take_heads(grad_ref, head)
        log_total = take_row(total_ref, head)
        inner = take_row(inner_ref, head)
        key_lanes = slice(head * HEAD, (head + 1) * HEAD)
        value_lanes = slice(KVD + head * HEAD, KVD + (head + 1) * HEAD)

        def step(
            index,
            total,
            query=query,
            grad=grad,
            log_total=log_total,
            inner=inner,
            key_lanes=key_lanes,
            value_lanes=value_lanes,
        ):
            rows = pl.ds(pl.multiple_of(index * CHUNK, CHUNK), CHUNK)
            key = packed_ref[rows, key_lanes]
            value = packed_ref[rows, value_lanes]
            bias = bias_ref[rows, :]
            scores = nt_dot(key, query) + jnp.concatenate([bias] * GROUP, axis=1)
            chance = jnp.exp(scores - log_total)
            grad_chance = nt_dot(value, grad)
            grad_scores = (chance * (grad_chance - inner)).astype(jnp.bfloat16)
            packed_out[rows, key_lanes] = plain_dot(grad_scores, query).astype(jnp.bfloat16)
            packed_out[rows, value_lanes] = plain_dot(
                chance.astype(jnp.bfloat16), grad
            ).astype(jnp.bfloat16)
            return total + tn_dot(key, grad_scores)

        start = jnp.zeros((HEAD, GROUP * tok_rows), jnp.float32)
        grad_query = lax.fori_loop(low, high, step, start) * (1.0 / math.sqrt(HEAD))
        for g in range(GROUP):
            at = GROUP * head + g
            query_out[at * HEAD : (at + 1) * HEAD, :] = grad_query[
                :, g * tok_rows : (g + 1) * tok_rows
            ]


IN_VMEM = pl.BlockSpec(memory_space=pltpu.VMEM)
IN_SMEM = pl.BlockSpec(memory_space=pltpu.SMEM)


def attend_forward(queries, packed, bias, chunk_range):
    tok_rows = queries.shape[0]
    return pl.pallas_call(
        forward_kernel,
        out_shape=(
            jax.ShapeDtypeStruct((HEADS * HEAD, tok_rows), jnp.float32),
            jax.ShapeDtypeStruct((HEADS, tok_rows), jnp.float32),
        ),
        in_specs=[IN_SMEM, IN_VMEM, IN_VMEM, IN_VMEM],
        out_specs=(IN_VMEM, IN_VMEM),
        compiler_params=pltpu.CompilerParams(vmem_limit_bytes=40 << 20),
        cost_estimate=pl.CostEstimate(
            flops=4 * 4096 * 128 * 960, bytes_accessed=8 << 20, transcendentals=4096 * 128 * 15
        ),
    )(chunk_range, queries, packed, bias)


def attend_backward(queries, packed, bias, chunk_range, log_total, inner, grad_mixed):
    tok_rows = queries.shape[0]
    return pl.pallas_call(
        backward_kernel,
        out_shape=(
            jax.ShapeDtypeStruct((HEADS * HEAD, tok_rows), jnp.float32),
            jax.ShapeDtypeStruct(packed.shape, jnp.bfloat16),
        ),
        in_specs=[IN_SMEM] + [IN_VMEM] * 6,
        out_specs=(IN_VMEM, IN_VMEM),
        compiler_params=pltpu.CompilerParams(vmem_limit_bytes=40 << 20),
        cost_estimate=pl.CostEstimate(
            flops=10 * 4096 * 128 * 960, bytes_accessed=13 << 20, transcendentals=4096 * 128 * 15
        ),
    )(chunk_range, queries, packed, bias, log_total, inner, grad_mixed)


def norm_backward(stream, gain, grad):
    return jax.vjp(root_norm, stream, gain)[1](grad)


def on_device(inputs, w_project, w_output, w_expand, w_contract, norm_gains, segments, cotangent):
    tok_rows = inputs.shape[1]
    width = inputs.shape[2]
    layers = w_project.shape[0]
    local_segment = segments[0]

    gain_row = jnp.pad(norm_gains[None, :], ((0, 0), (0, 240 - 30)))
    lead = jnp.concatenate([w_project[0].T, gain_row], axis=0)
    lead = gather_dp(pad_rows(lead, R_PROJECT, 0))
    segment_row = jnp.pad(
        local_segment.astype(jnp.bfloat16)[None, :], ((0, 0), (0, width - tok_rows))
    )
    lead = jnp.concatenate([lead[:51], segment_row, lead[52:]], axis=0)

    narrow = [w_expand[0].T, pad_rows(w_output[0].T, R_OUTPUT, 0)]
    narrow += [w_expand[1].T, pad_rows(w_output[1].T, R_OUTPUT, 0)]
    narrow += [pad_rows(w_project[1].T, R_PROJECT, 0)]
    narrow = gather_dp(jnp.concatenate(narrow, axis=0))
    wide = gather_dp(
        pad_rows(w_contract.transpose(0, 2, 1), R_OUTPUT, 1).reshape(2 * R_OUTPUT, 640)
    )
    bulk = jnp.concatenate(
        [narrow, pack_contract(wide[:R_OUTPUT]), pack_contract(wide[R_OUTPUT:])], axis=0
    )
    bulk = lax.all_gather(bulk, "seq")

    def take(start, rows, used):
        return bulk[:, start : start + rows][:, :used].reshape(32 * used, width)

    leads = gather_seq(lead)
    gains = (
        leads[:, 50, :].reshape(32, 4, 240)[:, :, :30].transpose(1, 0, 2).reshape(-1)
    ).astype(jnp.float32)
    all_segment = leads[:, 51, :tok_rows].reshape(-1).astype(jnp.int32)
    length = all_segment.shape[0]
    weights = [
        (
            leads[:, :50].reshape(1600, width),
            take(160, R_OUTPUT, 30),
            take(0, R_EXPAND, R_EXPAND),
            unpack_contract(bulk[:, 448:544]),
        ),
        (
            take(384, R_PROJECT, 50),
            take(352, R_OUTPUT, 30),
            take(192, R_EXPAND, R_EXPAND),
            unpack_contract(bulk[:, 544:640]),
        ),
    ]

    query_index = lax.axis_index("seq") * tok_rows + jnp.arange(tok_rows, dtype=jnp.int32)
    key_index = jnp.arange(length, dtype=jnp.int32)
    starts = jnp.sum((all_segment[None, :] < local_segment[:, None]).astype(jnp.int32), axis=1)
    position = (query_index - starts).astype(jnp.float32)
    angle = position[:, None] * frequencies(HEAD)[None, :]
    cosine = jnp.cos(angle)[:, None, :]
    sine = jnp.sin(angle)[:, None, :]
    allowed = (local_segment[None, :] == all_segment[:, None]) & (
        query_index[None, :] >= key_index[:, None]
    )
    bias = jnp.where(allowed, 0.0, MASKED).astype(jnp.float32)
    chunk_range = jnp.stack([starts[0] // CHUNK, query_index[-1] // CHUNK + 1])
    scale = 1.0 / math.sqrt(HEAD)
    stream = inputs[0].astype(jnp.float32)
    records = []
    for layer in range(layers):
        project, output, expand, contract = weights[layer]
        gain_attend = gains[2 * layer * width : (2 * layer + 1) * width]
        gain_feed = gains[(2 * layer + 1) * width : (2 * layer + 2) * width]
        normed = root_norm(stream, gain_attend).astype(jnp.bfloat16)
        projected = contract_cols(normed, project)
        queries = (
            (rotate(projected[:, :width].reshape(tok_rows, HEADS, HEAD), cosine, sine) * scale)
            .astype(jnp.bfloat16)
            .reshape(tok_rows, width)
        )
        keys = rotate(
            projected[:, width : width + KVD].reshape(tok_rows, KV_HEADS, HEAD), cosine, sine
        ).astype(jnp.bfloat16)
        values = projected[:, width + KVD :].astype(jnp.bfloat16)
        packed = gather_seq(
            jnp.concatenate([keys.reshape(tok_rows, KVD), values], axis=1)
        ).reshape(length, 2 * KVD)
        mixed_wide, log_total = attend_forward(queries, packed, bias, chunk_range)
        mixed_wide = mixed_wide.T
        mixed = mixed_wide.astype(jnp.bfloat16)
        middle = stream + contract_cols(mixed, output)
        normed_feed = root_norm(middle, gain_feed).astype(jnp.bfloat16)
        gate_up = contract_cols(normed_feed, expand)
        hidden = gated_unit(gate_up).astype(jnp.bfloat16)
        records.append(
            (
                stream,
                normed,
                queries,
                packed,
                log_total,
                mixed_wide,
                mixed,
                middle,
                normed_feed,
                gate_up,
                hidden,
            )
        )
        stream = middle + contract_cols(hidden, contract)
    block_output = stream.astype(jnp.bfloat16)[None]

    grad_stream = cotangent[0].astype(jnp.float32)
    bulk_grads = [None] * layers
    project_grads = [None] * layers
    gain_grads = [None] * layers
    for layer in reversed(range(layers)):
        project, output, expand, contract = weights[layer]
        (
            stream_in,
            normed,
            queries,
            packed,
            log_total,
            mixed_wide,
            mixed,
            middle,
            normed_feed,
            gate_up,
            hidden,
        ) = records[layer]
        gain_attend = gains[2 * layer * width : (2 * layer + 1) * width]
        gain_feed = gains[(2 * layer + 1) * width : (2 * layer + 2) * width]
        grad_low = grad_stream.astype(jnp.bfloat16)
        grad_contract = contract_rows(grad_low, hidden).astype(jnp.bfloat16)
        grad_hidden = plain_dot(grad_low, contract)
        grad_gate_up = jax.vjp(gated_unit, gate_up)[1](grad_hidden)[0].astype(jnp.bfloat16)
        grad_expand = contract_rows(grad_gate_up, normed_feed).astype(jnp.bfloat16)
        grad_feed = plain_dot(grad_gate_up, expand)
        grad_middle_part, grad_gain_feed = norm_backward(middle, gain_feed, grad_feed)
        grad_middle = grad_stream + grad_middle_part
        grad_middle_low = grad_middle.astype(jnp.bfloat16)
        grad_output = contract_rows(grad_middle_low, mixed).astype(jnp.bfloat16)
        bulk_grad = jnp.concatenate(
            [
                grad_expand.reshape(32, R_EXPAND, width),
                pad_rows(grad_output.reshape(32, 30, width), R_OUTPUT, 1),
                spread_contract(grad_contract),
            ],
            axis=1,
        )
        bulk_grads[layer] = lax.psum_scatter(bulk_grad, "seq", scatter_dimension=0)
        grad_mixed = plain_dot(grad_middle_low, output).astype(jnp.bfloat16)
        inner = jnp.sum(
            (grad_mixed.astype(jnp.float32) * mixed_wide).reshape(tok_rows, HEADS, HEAD), axis=2
        ).T
        grad_query, grad_packed = attend_backward(
            queries, packed, bias, chunk_range, log_total, inner, grad_mixed
        )
        grad_query = grad_query.T
        grad_local = reduce_seq(grad_packed.reshape(32, tok_rows, 2 * KVD))
        grad_query = rotate(grad_query.reshape(tok_rows, HEADS, HEAD), cosine, -sine)
        grad_key = rotate(grad_local[:, :KVD].reshape(tok_rows, KV_HEADS, HEAD), cosine, -sine)
        grad_projected = jnp.concatenate(
            [
                grad_query.reshape(tok_rows, width),
                grad_key.reshape(tok_rows, KVD),
                grad_local[:, KVD:],
            ],
            axis=1,
        ).astype(jnp.bfloat16)
        grad_project = contract_rows(grad_projected, normed).astype(jnp.bfloat16)
        grad_normed = plain_dot(grad_projected, project)
        grad_input_part, grad_gain_attend = norm_backward(stream_in, gain_attend, grad_normed)
        grad_stream = grad_middle + grad_input_part
        gain_grads[layer] = jnp.concatenate([grad_gain_attend, grad_gain_feed])
        project_rows = grad_project.reshape(32, 50, width)
        if layer == 0:
            gain_rows = (
                jnp.concatenate(gain_grads)
                .reshape(4, 32, 30)
                .transpose(1, 0, 2)
                .astype(jnp.bfloat16)
            )
            gain_rows = pad_rows(gain_rows, 240, 2).reshape(32, 1, width)
            project_rows = jnp.concatenate([project_rows, gain_rows], axis=1)
        project_rows = pad_rows(project_rows, R_PROJECT, 1)
        project_grads[layer] = reduce_dp(reduce_seq(project_rows))

    parts = [reduce_bulk(grad) for grad in bulk_grads]
    expand_out = jnp.stack([part[:R_EXPAND].T for part in parts])
    output_out = jnp.stack([part[R_EXPAND : R_EXPAND + 30].T for part in parts])
    contract_out = jnp.stack(
        [part[R_EXPAND + R_OUTPUT :].reshape(32, 720)[:30, :640].T for part in parts]
    )
    project_out = jnp.stack([part[:50].T for part in project_grads])
    gains_out = project_grads[0][50, :30]
    return (
        block_output,
        grad_stream[None],
        project_out,
        output_out,
        expand_out,
        contract_out,
        gains_out,
    )


def solution(mesh):
    in_specs = (
        P("dp", "seq", None),
        P(None, "dp", "seq"),
        P(None, "dp", "seq"),
        P(None, "dp", "seq"),
        P(None, "dp", "seq"),
        P(("dp", "seq")),
        P("dp", "seq"),
        P("dp", "seq", None),
    )
    out_specs = (
        P("dp", "seq", None),
        P("dp", "seq", None),
        P(None, "dp", "seq"),
        P(None, "dp", "seq"),
        P(None, "dp", "seq"),
        P(None, "dp", "seq"),
        P(("dp", "seq")),
    )
    return jax.shard_map(
        on_device, mesh=mesh, in_specs=in_specs, out_specs=out_specs, check_vma=False
    )
```

time: 1900 us -> 1150 us (0.61)
  waiting for transfers between devices: 1040 us -> 311 us
  blocking collectives: 352 us -> 103 us
  local copies, waits for them, and re-layouts: 146 us -> 358 us
  matrix products: 259 us -> 95 us
  starting transfers between devices: 18.1 us -> 130 us
  other arithmetic: 46.1 us -> 93.1 us
  Pallas kernels: 0 us -> 19 us
    unnamed x38 -> x6, waiting for transfers between devices: 359 us -> 0.1 us
    reduce_scatter x6 -> x2, waiting for transfers between devices: 284 us -> 0.04 us  [on_device(): bulk_grads[layer] = lax.psum_scatter(bulk_grad, 'seq', scatter_dimension=0)]
    unnamed x5 -> x0, blocking collectives: 226 us -> none
    all_gather x14 -> x4, waiting for transfers between devices: 399 us -> 203 us  [the longest x1 122 us: on_device(): bulk = lax.all_gather(bulk, 'seq')]
    reshape x6 -> x33, local copies, waits for them, and re-layouts: 23.5 us -> 166 us  [the longest x3 47.6 us: unpack_contract(): block.reshape(32, 3, 32, 960).transpose(0, 2, 1, 3).reshape(32, 32, 2880)]
    all_to_all x0 -> x7, starting transfers between devices: none -> 121 us  [the longest x3 58 us: reduce_seq(): lax.all_to_all(both, 'seq', 0, 0, axis_index_groups=PLANE, tiled=True)]
    all_to_all x0 -> x7, waiting for transfers between devices: none -> 96.3 us  [the longest x3 80.2 us: reduce_seq(): lax.all_to_all(both, 'seq', 0, 0, axis_index_groups=PLANE, tiled=True)]
    dot_general x38 -> x8, matrix products: 109 us -> 23.9 us  [contract_cols(): lax.dot_general(left, right, (((1,), (1,)), ((), ())), preferred_element_...]
  transfers between devices with their start and end apart: 31 -> 20, of which waited for: 19 -> 13; matrix products, arithmetic and copies ran while one was open for 17% -> 23% of each run, Pallas kernels for 0% -> 1%
where the time goes in v1:
time: 1150 us; the launch traced here: 1130 us
  local copies, waits for them, and re-layouts  358 us (31%)
  waiting for transfers between devices  311 us (27%)
  starting transfers between devices  130 us (11%)
  blocking collectives  103 us (9%)
  matrix products  95 us (8%)
  other arithmetic  93.1 us (8%)
  between operations  19.2 us (2%)
  Pallas kernels  19 us (2%)
    all_gather x1, waiting for transfers between devices, on_device(): bulk = lax.all_gather(bulk, 'seq')  122 us
    all_gather x3, waiting for transfers between devices, gather_seq(): plane = lax.all_gather(along_y, 'seq', axis_index_groups=RING_Z)  80.4 us
    all_to_all x3, waiting for transfers between devices, reduce_seq(): lax.all_to_all(both, 'seq', 0, 0, axis_index_groups=PLANE, tiled=True)  80.2 us
    all_to_all x3, starting transfers between devices, reduce_seq(): lax.all_to_all(both, 'seq', 0, 0, axis_index_groups=PLANE, tiled=True)  58 us
    all_to_all x2, starting transfers between devices, reduce_dp(): spread = lax.all_to_all(parts, 'dp', 0, 0, tiled=True)  56.2 us
    reshape x3, local copies, waits for them, and re-layouts, unpack_contract(): block.reshape(32, 3, 32, 960).transpose(0, 2, 1, 3).reshape(32, 32, 2880)  47.6 us
    all_gather x3, blocking collectives, gather_seq(): along_y = lax.all_gather(array, 'seq', axis_index_groups=RING_Y)  40.1 us
    reshape x2, local copies, waits for them, and re-layouts, spread_contract(): wide.reshape(32, 32, 3, 960).transpose(0, 2, 1, 3)  38.9 us
  transfers between devices with their start and end apart: 20, of which 13 were waited for; matrix products, arithmetic and copies ran while one was open for 23% of the time, Pallas kernels for 1%

profile of v1, /device:TPU:1, one launch (start us, length us, event | category | flops | bytes accessed | tf_op | source)
XLA Modules:
  0.0 1129.7 jit_solution(14924370925417378402)
XLA Ops:
  9.5 10.3 all-gather
  20.9 11.2 all-gather.1
  32.2 38.0 %all-gather.14.cloned.1.call-done = bf16[16,64,960]{2,1,0:T(8,128)(2,1)} async-done(((bf16[4,64,960]{2,1,0:T(8,128)(2,1)}), bf16[16,64,960]{2,1,0:T(8,128)(2,1)}) %all-gather.14.cloned.1.call-update) | async-done | bytes 1966096 | tf_op jit(solution)/shard_map/all_gather | solution.py:84
  91.9 14.5 %all-gather.3 = bf16[512,640]{0,1:T(8,128)(2,1)S(1)} all-gather(bf16[128,640]{0,1:T(8,128)(2,1)S(1)} %pad_maximum_fusion.15), channel_id=5, replica_groups={{0,2,4,6},{1,3,5,7},{8,10,12,14},{9,11,13,15},{16,18,20,22},{17,19,21,2..., dimensions={0}, use_global_device_ids=true | all-gather | bytes 819200 | tf_op jit(solution)/shard_map/all_gather | solution.py:83
  107.6 9.8 all_gather.69
  119.8 12.8 %all-gather.5 = bf16[1792,240]{1,0:T(8,128)(2,1)S(1)} all-gather(bf16[448,240]{1,0:T(8,128)(2,1)S(1)} %pad_dynamic-update-slice_fusion), channel_id=7, replica_groups=mesh['dp'=4,'seq'=32] {'dp'}, dimensions={0}, use_global_device_ids=true | all-gather | bytes 1075200 | tf_op jit(solution)/shard_map/all_gather | solution.py:122
  159.3 122.3 %all-gather.18.cloned.1.call-done = bf16[20480,960]{1,0:T(8,128)(2,1)} async-done(((bf16[640,960]{1,0:T(8,128)(2,1)}), bf16[20480,960]{1,0:T(8,128)(2,1)}) %all-gather.18.cloned.1.call-update) | async-done | bytes 39321616 | tf_op jit(solution)/shard_map/all_gather | solution.py:318
  290.8 11.2 fusion.87
  302.0 17.2 %fusion.88 = (bf16[32,160,960]{2,1,0:T(8,128)(2,1)}, bf16[32,160,960]{2,1,0:T(8,128)(2,1)}) fusion(bf16[32,640,960]{2,1,0:T(8,128)(2,1)} %bitcast.397), kind=kLoop, calls=%fused_computation.255 | loop fusion | bytes 39321600 | tf_op jit(solution)/shard_map/slice | solution.py:321
  330.5 12.3 %copy.442 = bf16[32,3,32,960]{3,1,2,0:T(4,128)(2,1)} copy(bf16[32,3,32,960]{3,2,1,0:T(8,128)(2,1)} %bitcast.408) | data formatting | bytes 11796480 | tf_op jit(solution)/shard_map/reshape | solution.py:132
  342.8 17.7 %reshape.482 = bf16[32,32,2880]{2,1,0:T(8,128)(2,1)} reshape(bf16[32,32,3,960]{3,2,1,0:T(4,128)(2,1)} %bitcast.402) | data formatting | bytes 11796480 | tf_op jit(solution)/shard_map/reshape | solution.py:132
  365.8 20.1 %reshape.483 = bf16[960,2560]{1,0:T(8,128)(2,1)} reshape(bf16[32,30,2560]{2,1,0:T(8,128)(2,1)} %slice.420) | data formatting | bytes 9830400 | tf_op jit(solution)/shard_map/reshape | solution.py:133
  386.0 8.0 fusion.80
  399.3 14.5 %all-gather.7 = bf16[512,640]{0,1:T(8,128)(2,1)} all-gather(bf16[128,640]{0,1:T(8,128)(2,1)S(1)} %pad_maximum_fusion.16), channel_id=9, replica_groups={{0,2,4,6},{1,3,5,7},{8,10,12,14},{9,11,13,15},{16,18,20,22},{17,19,21,2..., dimensions={0}, use_global_device_ids=true | all-gather | bytes 819200 | tf_op jit(solution)/shard_map/all_gather | solution.py:83
  416.0 35.8 %all-gather.20.cloned.1.call-done = bf16[16,128,640]{2,1,0:T(8,128)(2,1)} async-done(((bf16[4,128,640]{2,1,0:T(8,128)(2,1)}), bf16[16,128,640]{2,1,0:T(8,128)(2,1)}) %all-gather.20.cloned.1.call-update) | async-done | bytes 2621456 | tf_op jit(solution)/shard_map/all_gather | solution.py:84
  456.5 12.1 %copy.373 = bf16[32,32,3,960]{3,2,1,0:T(4,128)(2,1)} copy(bf16[32,32,3,960]{3,1,2,0:T(8,128)(2,1)} %bitcast.407) | data formatting | bytes 11796480 | tf_op jit(solution)/shard_map/transpose | solution.py:132
  468.6 17.7 %reshape.490 = bf16[32,32,2880]{2,1,0:T(8,128)(2,1)} reshape(bf16[32,32,3,960]{3,2,1,0:T(4,128)(2,1)} %copy.373) | data formatting | bytes 11796480 | tf_op jit(solution)/shard_map/reshape | solution.py:132
  562.1 19.4 %reshape.520 = bf16[32,32,3,960]{3,2,1,0:T(4,128)(2,1)} reshape(bf16[32,32,2880]{2,1,0:T(8,128)(2,1)} %pad.99) | data formatting | bytes 11796480 | tf_op jit(solution)/shard_map/reshape | solution.py:138
  581.5 9.2 copy.404
  590.7 14.3 %copy.403 = bf16[5120,960]{1,0:T(8,128)(2,1)} copy(bf16[5120,960]{0,1:T(8,128)(2,1)} %convolution_convert_fusion) | data formatting | bytes 19660800 | tf_op jit(solution)/shard_map/convert_element_type | solution.py:427
  605.0 18.3 %fusion.6 = bf16[32,288,960]{2,1,0:T(8,128)(2,1)} fusion(bf16[32,30,960]{2,1,0:T(8,128)(2,1)} %reshape.518, bf16[32,96,960]{2,1,0:T(8,128)(2,1)} %bitcast.406, bf16[32,160,960]{2,1,0:T(8,128)(2,1)} %bitcast.392), kind=kLoop, calls=%fused_computation.8 | loop fusion | flops 88473600 | bytes 35266560 | tf_op jit(solution)/shard_map/concatenate | solution.py:433
  646.2 33.2 %all-to-all-start = ((bf16[16,128,640]{2,1,0:T(8,128)(2,1)}), bf16[16,128,640]{2,1,0:T(8,128)(2,1)}, u32[]{:S(2)}, u32[]{:S(2)}) async-start(bf16[16,128,640]{2,1,0:T(8,128)(2,1)} %fusion.10), calls=%async_computation | async-start | bytes 5242880 | tf_op jit(solution)/shard_map/all_to_all | solution.py:99
  680.7 42.6 %all-to-all-done = bf16[16,128,640]{2,1,0:T(8,128)(2,1)} async-done(((bf16[16,128,640]{2,1,0:T(8,128)(2,1)}), bf16[16,128,640]{2,1,0:T(8,128)(2,1)}, u32[]{:S(2)}, u32[]{:S(2)}) %all-to-all-start) | async-done | bytes 2621472 | tf_op jit(solution)/shard_map/all_to_all | solution.py:99
  770.1 19.4 %reshape.510 = bf16[32,32,3,960]{3,2,1,0:T(4,128)(2,1)} reshape(bf16[32,32,2880]{2,1,0:T(8,128)(2,1)} %pad.96) | data formatting | bytes 11796480 | tf_op jit(solution)/shard_map/reshape | solution.py:138
  789.5 9.5 copy.398
  804.3 14.3 %copy.397 = bf16[5120,960]{1,0:T(8,128)(2,1)} copy(bf16[5120,960]{0,1:T(8,128)(2,1)} %convolution_convert_fusion.1) | data formatting | bytes 19660800 | tf_op jit(solution)/shard_map/convert_element_type | solution.py:427
  818.6 18.3 %fusion.4 = bf16[32,288,960]{2,1,0:T(8,128)(2,1)} fusion(bf16[32,30,960]{2,1,0:T(8,128)(2,1)} %reshape.508, bf16[32,96,960]{2,1,0:T(8,128)(2,1)} %bitcast.405, bf16[32,160,960]{2,1,0:T(8,128)(2,1)} %bitcast.393), kind=kLoop, calls=%fused_computation.6 | loop fusion | flops 88473600 | bytes 35266560 | tf_op jit(solution)/shard_map/concatenate | solution.py:433
  862.7 21.1 %all-to-all-start.1 = ((bf16[16,128,640]{2,1,0:T(8,128)(2,1)}), bf16[16,128,640]{2,1,0:T(8,128)(2,1)}, u32[]{:S(2)}, u32[]{:S(2)}) async-start(bf16[16,128,640]{2,1,0:T(8,128)(2,1)} %fusion.9), calls=%async_computation.1 | async-start | bytes 5242880 | tf_op jit(solution)/shard_map/all_to_all | solution.py:99
  906.7 16.9 %all-to-all-done.1 = bf16[16,128,640]{2,1,0:T(8,128)(2,1)} async-done(((bf16[16,128,640]{2,1,0:T(8,128)(2,1)}), bf16[16,128,640]{2,1,0:T(8,128)(2,1)}, u32[]{:S(2)}, u32[]{:S(2)}) %all-to-all-start.1) | async-done | bytes 2621472 | tf_op jit(solution)/shard_map/all_to_all | solution.py:99
  959.2 30.5 %all_to_all.40 = bf16[16,64,960]{2,1,0:T(8,128)(2,1)S(1)} all-to-all(bf16[16,64,960]{2,1,0:T(8,128)(2,1)S(1)} %fusion.13), channel_id=1, replica_groups={{0,2,4,6,8,10,12,14,16,18,20,22,24,26,28,30},{1,3,5,7,9,11,13,15,17,19,..., dimensions={0} | all-to-all | bytes 3932160 | tf_op jit(solution)/shard_map/all_to_all | solution.py:99
  990.9 52.0 %all-to-all-start.5 = ((bf16[4,64,240]{2,1,0:T(8,128)(2,1)}), bf16[4,64,240]{2,1,0:T(8,128)(2,1)S(1)}, u32[]{:S(2)}, u32[]{:S(2)}) async-start(bf16[4,64,240]{2,1,0:T(8,128)(2,1)} %copy.396), calls=%async_computation.5 | async-start | bytes 262144 | tf_op jit(solution)/shard_map/all_to_all | solution.py:106
  1057.8 20.7 %all-to-all-done.2 = bf16[16,64,960]{2,1,0:T(8,128)(2,1)S(1)} async-done(((bf16[16,64,960]{2,1,0:T(8,128)(2,1)}), bf16[16,64,960]{2,1,0:T(8,128)(2,1)S(1)}, u32[]{:S(2)}, u32[]{:S(2)}) %all-to-all-start.2) | async-done | bytes 1966112 | tf_op jit(solution)/shard_map/all_to_all | solution.py:99
  (448 shorter events, 385.4 us)
Async XLA Ops:
  7.2 64.2 %copy-start.31 = (bf16[1,128,960]{1,2,0:T(8,128)(2,1)S(1)}, bf16[1,128,960]{1,2,0:T(8,128)(2,1)}, u32[]{:S(2)}) copy-start(bf16[1,128,960]{1,2,0:T(8,128)(2,1)} %param.8) | copy-start | bytes 737284
  7.2 63.0 %all-gather.14.cloned.1.call-start = ((), (), s32[]{:S(2)}) async-start(), calls=%async_computation.12 | async-start | bytes 2621440 | tf_op jit(solution)/shard_map/all_gather | solution.py:84
  32.1 111.0 %all-gather.16.cloned.1.call-start = ((), (), s32[]{:S(2)}) async-start(), calls=%async_computation.13 | async-start | bytes 3276800 | tf_op jit(solution)/shard_map/all_gather | solution.py:84
  70.2 4.7 collective-permute-start
  107.5 174.1 %all-gather.18.cloned.1.call-start = ((), (), s32[]{:S(2)}) async-start(), calls=%async_computation.14 | async-start | bytes 43253760 | tf_op jit(solution)/shard_map/all_gather | solution.py:318
  136.5 315.3 %all-gather.20.cloned.1.call-start = ((), (), s32[]{:S(2)}) async-start(), calls=%async_computation.15 | async-start | bytes 3276800 | tf_op jit(solution)/shard_map/all_gather | solution.py:84
  143.2 5.9 collective-permute-start.1
  148.0 238.0 %copy-start.49 = (f32[960]{0:T(1024)}, f32[960]{0:T(1024)S(1)}, u32[]{:S(2)}) copy-start(f32[960]{0:T(1024)S(1)} %slice.337) | copy-start | bytes 11524
  330.5 65.4 %copy-start.12 = (f32[128,960]{0,1:T(8,128)}, f32[128,960]{0,1:T(8,128)S(1)}, u32[]{:S(2)}) copy-start(f32[128,960]{0,1:T(8,128)S(1)} %get-tuple-element.127) | copy-start | bytes 1474564
  330.5 55.5 %copy-start.65 = (f32[128]{0:T(128)}, f32[128]{0:T(128)S(1)}, u32[]{:S(2)}) copy-start(f32[128]{0:T(128)S(1)} %fusion.69) | copy-start | bytes 1540
  399.2 57.3 %copy-start.38 = (f32[128,1600]{0,1:T(8,128)}, f32[128,1600]{0,1:T(8,128)S(1)}, u32[]{:S(2)}) copy-start(f32[128,1600]{0,1:T(8,128)S(1)} %fusion.81) | copy-start | bytes 2457604
  399.2 53.3 %copy-start.57 = (f32[32,30]{1,0:T(8,128)S(1)}, f32[32,30]{1,0:T(8,128)}, u32[]{:S(2)}) copy-start(f32[32,30]{1,0:T(8,128)} %get-tuple-element.80) | copy-start | bytes 11524
  416.0 672.8 %reduce-scatter.5.cloned.1.call-start = ((), (), s32[]{:S(2)}) async-start(), calls=%async_computation.11 | async-start | bytes 19464192 | tf_op jit(solution)/shard_map/reduce_scatter | solution.py:441
  451.8 47.7 %collective-permute-start.2 = (bf16[4,4,128,640]{3,2,1,0:T(8,128)(2,1)}, bf16[4,4,128,640]{3,2,1,0:T(8,128)(2,1)}, u32[]{:S(2)}, u32[]{:S(2)}) collective-permute-start(bf16[4,4,128,640]{3,2,1,0:T(8,128)(2,1)} %bitcast.420), channel_id=1, source_target_pairs={{0,1},{1,0},{2,3},{3,2},{4,5},{5,4},{6,7},{7,6},{8,9},{9,8},{10,11... | collective-permute-start | bytes 7864328 | tf_op jit(solution)/shard_map/ppermute | solution.py:79
  638.6 5.0 collective-permute-start.3
  646.2 33.6 %copy-start.45 = (f32[128,32]{0,1:T(8,128)S(1)}, f32[128,32]{0,1:T(8,128)}, u32[]{:S(2)}) copy-start(f32[128,32]{0,1:T(8,128)} %get-tuple-element.123) | copy-start | bytes 49156
  646.2 77.1 %all-to-all-start = ((bf16[16,128,640]{2,1,0:T(8,128)(2,1)}), bf16[16,128,640]{2,1,0:T(8,128)(2,1)}, u32[]{:S(2)}, u32[]{:S(2)}) async-start(bf16[16,128,640]{2,1,0:T(8,128)(2,1)} %fusion.10), calls=%async_computation | async-start | bytes 5242880 | tf_op jit(solution)/shard_map/all_to_all | solution.py:99
  679.4 425.0 %reduce-scatter.3.cloned.1.call-start = ((), (), s32[]{:S(2)}) async-start(), calls=%async_computation.10 | async-start | bytes 19464192 | tf_op jit(solution)/shard_map/reduce_scatter | solution.py:441
  680.0 47.6 %copy-start.21 = (f32[128,960]{0,1:T(8,128)S(1)}, f32[128,960]{0,1:T(8,128)}, u32[]{:S(2)}) copy-start(f32[128,960]{0,1:T(8,128)} %copy-done.19) | copy-start | bytes 1474564
  851.5 8.6 collective-permute-start.4
  862.7 23.2 %copy-start.47 = (bf16[128,320]{0,1:T(8,128)(2,1)S(1)}, bf16[128,320]{0,1:T(8,128)(2,1)}, u32[]{:S(2)}) copy-start(bf16[128,320]{0,1:T(8,128)(2,1)} %copy-done.46) | copy-start | bytes 245764
  862.7 60.9 %all-to-all-start.1 = ((bf16[16,128,640]{2,1,0:T(8,128)(2,1)}), bf16[16,128,640]{2,1,0:T(8,128)(2,1)}, u32[]{:S(2)}, u32[]{:S(2)}) async-start(bf16[16,128,640]{2,1,0:T(8,128)(2,1)} %fusion.9), calls=%async_computation.1 | async-start | bytes 5242880 | tf_op jit(solution)/shard_map/all_to_all | solution.py:99
  905.3 50.8 %collective-permute-start.6 = (bf16[16,64,960]{2,1,0:T(8,128)(2,1)}, bf16[16,64,960]{2,1,0:T(8,128)(2,1)}, u32[]{:S(2)}, u32[]{:S(2)}) collective-permute-start(bf16[16,64,960]{2,1,0:T(8,128)(2,1)} %select_bitcast_fusion.6), channel_id=1, source_target_pairs={{0,1},{1,0},{2,3},{3,2},{4,5},{5,4},{6,7},{7,6},{8,9},{9,8},{10,11... | collective-permute-start | bytes 5898248 | tf_op jit(solution)/shard_map/ppermute | solution.py:79
  905.9 25.9 %copy-start.16 = (bf16[1600,960]{1,0:T(8,128)(2,1)S(1)}, bf16[1600,960]{1,0:T(8,128)(2,1)}, u32[]{:S(2)}) copy-start(bf16[1600,960]{1,0:T(8,128)(2,1)} %copy-done.15) | copy-start | bytes 9216004
  906.0 25.9 %copy-start.32 = (bf16[1,128,960]{1,2,0:T(8,128)(2,1)S(1)}, bf16[1,128,960]{1,2,0:T(8,128)(2,1)}, u32[]{:S(2)}) copy-start(bf16[1,128,960]{1,2,0:T(8,128)(2,1)} %param.8) | copy-start | bytes 737284
  954.2 88.7 %collective-permute-start.5 = (bf16[16,64,960]{2,1,0:T(8,128)(2,1)}, bf16[16,64,960]{2,1,0:T(8,128)(2,1)}, u32[]{:S(2)}, u32[]{:S(2)}) collective-permute-start(bf16[16,64,960]{2,1,0:T(8,128)(2,1)} %select_bitcast_fusion.7), channel_id=1, source_target_pairs={{0,1},{1,0},{2,3},{3,2},{4,5},{5,4},{6,7},{7,6},{8,9},{9,8},{10,11... | collective-permute-start | bytes 5898248 | tf_op jit(solution)/shard_map/ppermute | solution.py:79
  990.9 57.8 %all-to-all-start.5 = ((bf16[4,64,240]{2,1,0:T(8,128)(2,1)}), bf16[4,64,240]{2,1,0:T(8,128)(2,1)S(1)}, u32[]{:S(2)}, u32[]{:S(2)}) async-start(bf16[4,64,240]{2,1,0:T(8,128)(2,1)} %copy.396), calls=%async_computation.5 | async-start | bytes 262144 | tf_op jit(solution)/shard_map/all_to_all | solution.py:106
  1049.4 29.2 %all-to-all-start.2 = ((bf16[16,64,960]{2,1,0:T(8,128)(2,1)}), bf16[16,64,960]{2,1,0:T(8,128)(2,1)S(1)}, u32[]{:S(2)}, u32[]{:S(2)}) async-start(bf16[16,64,960]{2,1,0:T(8,128)(2,1)} %fusion.14), calls=%async_computation.2 | async-start | bytes 4194304 | tf_op jit(solution)/shard_map/all_to_all | solution.py:99
  1057.7 26.2 %copy-start.27 = (f32[128,960]{0,1:T(8,128)S(1)}, f32[128,960]{0,1:T(8,128)}, u32[]{:S(2)}) copy-start(f32[128,960]{0,1:T(8,128)} %copy-done.25) | copy-start | bytes 1474564
  1079.8 9.0 all-to-all-start.3
  1093.5 10.7 all-to-all-start.7
  1109.1 10.7 all-to-all-start.6
  (78 other events, 540.8 us)
Sparse Core Ops, SparseCore 0:
  32.2 37.8 all-gather.13
  107.6 35.4 all-gather.15
  145.4 136.1 all-gather.17
  416.1 35.6 all-gather.19
  623.5 172.0 reduce-scatter.4
  837.1 177.3 reduce-scatter.2
